TPU v7x, 256 devices: a whole 4x4x8 slice. The times are simulated.
256 devices in a mesh: sector: 16 (over y, x), box: 16 (over z, core).
Axes of the slice: x: 4, y: 4, z: 8, core: 2. Of those that a mesh axis runs over, the one named last changes fastest.
Arguments:
- positions: float32 [3, 16, 1024, 128], P(None, 'sector', 'box'), may hold values from -0.9 to 0.9
- strengths: float32 [3, 16, 1024, 128], P(None, 'sector', 'box'), may hold values from -6 to 6
- counts: int32 [16, 1024], P('sector', 'box'), may hold values from 1 to 128
- cross_slot: int32 [16, 4096], P('sector', 'box'), may hold values from 0 to 8191, as said below
- arrive_box: int32 [16, 4096], P('sector', 'box'), may hold values from 0 to 63
- il_source: int32 [16, 1024, 16], P('sector', 'box'), may hold values from 0 to 63
- il_class: int32 [16, 1024, 16], P('sector', 'box'), may hold values from 0 to 3
- m2m: bfloat16 [4, 441, 441], replicated, may hold values from -0.125 to 0.125
- m2l_leaf: bfloat16 [4, 441, 441], replicated, may hold values from -0.0625 to 0.0625
- tree_up: bfloat16 [2, 441, 441], replicated, may hold values from -0.21875 to 0.21875
- tree_m2l: bfloat16 [2, 441, 441], replicated, may hold values from -0.25 to 0.25
- m2l_sector: bfloat16 [15, 441, 441], replicated, may hold values from -0.078125 to 0.078125
Outputs:
- new_positions: float32 [3, 16, 1024, 128], P(None, 'sector', 'box')
- velocity: float32 [3, 16, 1024, 128], P(None, 'sector', 'box')
Inputs may be any that keep to these rules, and one draw needn't show every extreme that they name: `cross_slot`: within one block's 256 entries the slot numbers are distinct; a slot beyond its box's count carries nothing.
All inputs are finite; a program needn't handle non-finite values.
Results may differ from a plain program's by a relative error of at most 0.006.
Values may be sent and summed in bfloat16 or wider, within the bound.
A program may use at most 128 MiB of HBM per device.

v0:
```python
import math
import jax
import jax.numpy as jnp
from jax import lax
from jax.sharding import PartitionSpec as P

TERMS = 21
LEVELS_DEV = 3
NCLASS = 4
DELTA_SQ = 0.25
TIME_STEP = 0.02
INV_FOUR_PI = 1.0 / (4.0 * math.pi)
HIGHEST_PRECISION = lax.Precision.HIGHEST
OFFSETS = ((0.0, 0.0, 0.0), (0.0, 0.0, -2.0), (0.0, 0.0, 2.0), (-2.0, 0.0, 0.0), (2.0, 0.0, 0.0))


def with_halo(array, sides, width, wrap):
    for axis, dim in sides:
        devices, length = (lax.axis_size(axis), array.shape[dim])
        up = [(i, (i + 1) % devices) for i in range(devices if wrap else devices - 1)]
        down = [(j, i) for i, j in up]
        last = lax.slice_in_dim(array, length - width, length, axis=dim)
        first = lax.slice_in_dim(array, 0, width, axis=dim)
        before = lax.ppermute(last, axis, up)
        after = lax.ppermute(first, axis, down)
        array = jnp.concatenate([before, array, after], axis=dim)
    return array


def partner_2(block, axis, distance):
    count = lax.axis_size(axis)
    route = []
    for low in range(count):
        high = low | 1 << distance
        if high != low and high < count:
            route += [(low, high), (high, low)]
    return lax.ppermute(block, axis, route)


def passed_along(array, axis, by):
    devices = lax.axis_size(axis)
    return lax.ppermute(array, axis, [(i, (i + by) % devices) for i in range(devices)])


def chebyshev(coordinate):
    scaled = 0.5 * coordinate
    series = [jnp.ones_like(scaled), scaled]
    for order in range(2, TERMS):
        series.append(2.0 * scaled * series[-1] - series[-2])
    return jnp.stack(series[:TERMS])


def multipoles(cheb_a, cheb_b, weights):
    weighted = weights[:, None] * cheb_a[None]
    return jnp.einsum("cjnp,knp->ncjk", weighted, cheb_b, precision=HIGHEST_PRECISION)


def evaluate(local, cheb_a, cheb_b):
    shaped = local.reshape(local.shape[0], 3, TERMS, TERMS)
    partial_sum = jnp.einsum("ncjk,knp->cjnp", shaped, cheb_b, precision=HIGHEST_PRECISION)
    return jnp.sum(partial_sum * cheb_a[None], axis=1) / TERMS


def pair_velocity(target, source, weight, offset):
    delta_x = target[0][:, :, None] - (source[0][:, None, :] + offset[0])
    delta_y = target[1][:, :, None] - (source[1][:, None, :] + offset[1])
    delta_z = target[2][:, :, None] - (source[2][:, None, :] + offset[2])
    radius_sq = delta_x * delta_x + delta_y * delta_y + delta_z * delta_z + DELTA_SQ
    inverse = INV_FOUR_PI / (radius_sq * jnp.sqrt(radius_sq))
    weight_x = weight[0][:, None, :]
    weight_y = weight[1][:, None, :]
    weight_z = weight[2][:, None, :]
    speed_x = jnp.sum(inverse * (weight_y * delta_z - weight_z * delta_y), axis=2)
    speed_y = jnp.sum(inverse * (weight_z * delta_x - weight_x * delta_z), axis=2)
    speed_z = jnp.sum(inverse * (weight_x * delta_y - weight_y * delta_x), axis=2)
    return jnp.stack([speed_x, speed_y, speed_z])


def near_field(places, weights):
    box_count, slots = (places.shape[1], places.shape[2])
    stacked = jnp.concatenate([places, weights], axis=0)[:, None]
    beside = with_halo(stacked.astype(jnp.bfloat16), (("sector", 1),), 1, True).astype(
        stacked.dtype
    )
    along = with_halo(stacked.astype(jnp.bfloat16), (("box", 2),), 1, False).astype(stacked.dtype)
    sources = [stacked[:, 0], along[:, 0, :box_count], along[:, 0, 2:], beside[:, 0], beside[:, 2]]
    block = math.gcd(box_count, 64)
    block_count = box_count // block

    def arrange(array):
        return array.reshape(array.shape[0], block_count, block, slots).transpose(1, 0, 2, 3)

    inputs = (arrange(places),) + tuple((arrange(item) for item in sources))

    def block_velocity(items):
        summed = jnp.zeros_like(items[0])
        for index in range(5):
            summed = summed + pair_velocity(
                items[0], items[1 + index][:3], items[1 + index][3:], OFFSETS[index]
            )
        return summed

    result = lax.map(block_velocity, inputs)
    return result.transpose(1, 0, 2, 3).reshape(3, box_count, slots)


def merge_pair(current, partner, side_bit, tree_up):
    lower_node = jnp.where(side_bit == 0, current, partner)
    upper_node = jnp.where(side_bit == 0, partner, current)
    merged = jnp.dot(lower_node, tree_up[0], preferred_element_type=jnp.float32) + jnp.dot(
        upper_node, tree_up[1], preferred_element_type=jnp.float32
    )
    return merged.astype(jnp.bfloat16)


def far_field(
    places,
    weights,
    arrival_terms,
    il_source,
    il_class,
    m2m,
    m2l_leaf,
    tree_up,
    tree_m2l,
    m2l_sector,
):
    box_count = places.shape[1]
    coef = TERMS * TERMS
    cheb_a = chebyshev(places[0])
    cheb_b = chebyshev(places[1])
    leaf = (
        (multipoles(cheb_a, cheb_b, weights) + arrival_terms)
        .reshape(box_count, 3, coef)
        .astype(jnp.bfloat16)
    )
    upward = leaf
    for depth in range(LEVELS_DEV):
        grouped = upward.reshape(-1, 4, 3, coef)
        upward = jnp.einsum(
            "gocx,oxy->gcy", grouped, m2m, preferred_element_type=jnp.float32
        ).astype(jnp.bfloat16)
    block_root = upward[0]
    box_index = lax.axis_index("box")
    depth_count = lax.axis_size("box").bit_length() - 1
    siblings = []
    side_bits = []
    current = block_root
    for depth in range(depth_count):
        partner = partner_2(current, "box", depth)
        side_bit = box_index >> depth & 1
        siblings.append(partner)
        side_bits.append(side_bit)
        current = merge_pair(current, partner, side_bit, tree_up)
    sector_index = lax.axis_index("sector")
    sector_count = lax.axis_size("sector")
    piece = lax.all_gather(current[None], "sector", axis=0, tiled=True)
    source_ids = jnp.arange(piece.shape[0], dtype=jnp.int32)
    distance = (source_ids - sector_index) % sector_count
    matrices = m2l_sector[jnp.maximum(distance - 1, 0)]
    masked_piece = jnp.where((distance != 0)[:, None, None], piece, jnp.zeros_like(piece))
    far_sum = jnp.einsum("ncx,nxy->cy", masked_piece, matrices, preferred_element_type=jnp.float32)
    local = far_sum.astype(jnp.bfloat16)
    for depth in reversed(range(depth_count)):
        up_side = lax.dynamic_index_in_dim(tree_up, side_bits[depth], 0, keepdims=False)
        cross_side = lax.dynamic_index_in_dim(tree_m2l, side_bits[depth], 0, keepdims=False)
        downward = jnp.einsum(
            "cy,xy->cx", local, up_side, preferred_element_type=jnp.float32
        ) + jnp.dot(siblings[depth], cross_side, preferred_element_type=jnp.float32)
        local = downward.astype(jnp.bfloat16)
    parent_local = local[None]
    child = jnp.zeros((box_count, 3, coef), jnp.float32)
    for depth in range(LEVELS_DEV):
        child = jnp.einsum(
            "gcy,oxy->gocx", parent_local, m2m, preferred_element_type=jnp.float32
        ).reshape(-1, 3, coef)
        if depth + 1 < LEVELS_DEV:
            parent_local = child.astype(jnp.bfloat16)
    box_ids = jnp.arange(box_count, dtype=jnp.int32)
    source_hit = (il_source[0][:, :, None] == box_ids[None, None, :]).astype(jnp.bfloat16)
    class_hit = (
        il_class[0][:, :, None] == jnp.arange(NCLASS, dtype=jnp.int32)[None, None, :]
    ).astype(jnp.bfloat16)
    pair_counts = jnp.einsum(
        "bic,bis->cbs", class_hit, source_hit, preferred_element_type=jnp.float32
    ).astype(jnp.bfloat16)
    presum = jnp.einsum(
        "cbs,sx->cbx",
        pair_counts,
        leaf.reshape(box_count, 3 * coef),
        preferred_element_type=jnp.float32,
    )
    presum = presum.astype(jnp.bfloat16).reshape(NCLASS, box_count * 3, coef)
    translated = jnp.einsum(
        "cnx,cxy->ny", presum, m2l_leaf, preferred_element_type=jnp.float32
    ).reshape(box_count, 3, coef)
    return evaluate(child + translated, cheb_a, cheb_b)


def per_device(
    positions,
    strengths,
    counts,
    cross_slot,
    arrive_box,
    il_source,
    il_class,
    m2m,
    m2l_leaf,
    tree_up,
    tree_m2l,
    m2l_sector,
):
    box_count, slots = (positions.shape[2], positions.shape[3])
    slot_ids = jnp.arange(slots, dtype=jnp.int32)
    present = (slot_ids[None, :] < counts[0][:, None]).astype(jnp.float32)
    crossing = cross_slot[0]
    departed = jnp.zeros((box_count * slots,), jnp.float32).at[crossing].set(1.0)
    live = present * (1.0 - departed.reshape(box_count, slots))
    flat_places = positions[:, 0].reshape(3, box_count * slots)
    flat_strength = strengths[:, 0].reshape(3, box_count * slots)
    leave_present = present.reshape(-1)[crossing]
    leaving = jnp.concatenate(
        [flat_places[:, crossing], flat_strength[:, crossing] * leave_present[None]], axis=0
    )
    arrived = passed_along(leaving, "sector", 1)
    arrive_cheb_a = chebyshev(arrived[0][:, None])
    arrive_cheb_b = chebyshev(arrived[1][:, None])
    arrival_each = multipoles(arrive_cheb_a, arrive_cheb_b, arrived[3:6][:, :, None])
    box_ids = jnp.arange(box_count, dtype=jnp.int32)
    landing = (arrive_box[0][None, :] == box_ids[:, None]).astype(jnp.float32)
    arrival_terms = jnp.dot(
        landing, arrival_each.reshape(landing.shape[1], -1), precision=HIGHEST_PRECISION
    )
    arrival_terms = arrival_terms.reshape(box_count, 3, TERMS, TERMS)
    places = positions[:, 0]
    weights = strengths[:, 0] * live[None]
    velocity = jnp.zeros_like(places)
    for substep in range(2):
        near = near_field(places, weights)
        far = far_field(
            places,
            weights,
            arrival_terms,
            il_source,
            il_class,
            m2m,
            m2l_leaf,
            tree_up,
            tree_m2l,
            m2l_sector,
        )
        velocity = near + far
        places = places + TIME_STEP * velocity
    return (places[:, None], velocity[:, None])


def solution(mesh):
    placed = (
        P(None, "sector", "box", None),
        P(None, "sector", "box", None),
        P("sector", "box"),
        P("sector", "box"),
        P("sector", "box"),
        P("sector", "box", None),
        P("sector", "box", None),
        P(),
        P(),
        P(),
        P(),
        P(),
    )
    return jax.shard_map(
        per_device,
        mesh=mesh,
        in_specs=placed,
        out_specs=(P(None, "sector", "box", None), P(None, "sector", "box", None)),
        check_vma=False,
    )
```

profile of v0, /device:TPU:2, one launch (start us, length us, event | category | flops | bytes accessed | tf_op | source)
XLA Modules:
  0.0 371.9 jit_solution(226998493648815140)
XLA Ops:
  9.0 3.4 copy.326
  12.5 2.7 copy.325
  15.2 3.0 gather_fusion.1
  20.1 2.9 gather_fusion
  26.3 3.6 collective-permute-start
  36.4 6.5 %constant_dynamic-slice_fusion.1 = (bf16[1,441,441]{2,0,1:T(2,128)(2,1)}, bf16[1,441,441]{2,0,1:T(2,128)(2,1)}, bf16[1,441,441]{2,0,1:T(2,128)(2,1)}, bf16[1,441...) fusion(bf16[2,441,441]{2,0,1:T(2,128)(2,1)S(1)} %copy-done.2, ...), kind=kLoop, calls=%fused_computation.812 | loop fusion | bytes 4667560 | tf_op jit(solution)/shard_map/jit(dynamic_index_in_dim)/dynamic_slice | solution.py:165
  42.9 4.9 %constant_dynamic-slice_fusion = (bf16[1,441,441]{2,0,1:T(2,128)(2,1)}, bf16[1,441,441]{2,0,1:T(2,128)(2,1)}, bf16[1,441,441]{2,0,1:T(2,128)(2,1)}, bf16[1,441,441]{2,0,1:T(2,128)(2,1)}) fusion(bf16[2,441,441]{2,0,1:T(2,128)(2,1)S(1)} %copy-done.3, s32[]{:T(128)S(6)} %select_n.162, s32[]{:T(128)S(6)} %select_n.161, s32[]{:T(128)S(6)} %select_n.160, ...), kind=kLoop, calls=%fused_computation.811 | loop fusion | bytes 3111712 | tf_op jit(solution)/shard_map/jit(dynamic_index_in_dim)/dynamic_slice | solution.py:166
  50.7 5.4 %fusion.134 = f32[64,3,21,21]{3,2,1,0:T(8,128)S(1)} fusion(f32[21,64,128]{2,0,1:T(8,128)} %copy.323, f32[3,64,128]{2,0,1:T(4,128)} %copy.322, f32[21,64,128,1]{2,1,0,3:T(8,128)} %bitcast.1389), kind=kOutput, calls=%fused_computation.243 | convolution fusion | flops 130572288 | bytes 1813248 | tf_op jit(solution)/shard_map/cjnp,knp->ncjk/dot_general | solution.py:55
  58.2 7.0 %gather_fusion.3 = bf16[16,441,441]{2,1,0:T(8,128)(2,1)} fusion(bf16[15,441,441]{2,1,0:T(8,128)(2,1)} %param.23, s32[1024]{0:T(1024)} %pad_clamp_fusion), kind=kCustom, calls=%fused_computation.3 | custom fusion | bytes 12446848 | tf_op jit(solution)/shard_map/gather | solution.py:160
  67.9 2.9 dot_general.193
  70.8 3.3 add_convert_fusion.1
  75.8 2.8 convert_element_type.236
  87.5 4.4 %collective-permute-start.7 = (bf16[3,441]{1,0:T(4,128)(2,1)S(1)}, bf16[3,441]{1,0:T(4,128)(2,1)S(1)}, u32[]{:S(2)}, u32[]{:S(2)}) collective-permute-start(bf16[3,441]{1,0:T(4,128)(2,1)S(1)} %fusion.240), channel_id=1, source_target_pairs={{0,4},{4,0},{1,5},{5,1},{2,6},{6,2},{3,7},{7,3},{8,12},{12,8},{9,1... | collective-permute-start | bytes 7946 | tf_op jit(solution)/shard_map/ppermute | solution.py:37
  91.9 25.5 %fusion.45 = (f32[64,128]{1,0:T(8,128)}, f32[64,128]{1,0:T(8,128)}, f32[64,128]{1,0:T(8,128)}, f32[64,128]{1,0:T(8,128)}, f32[64,128]{1,0:T(8,128)}, /*index=5*/f32[64,128]{1,0:T(8,128)}) fusion(f32[64,128]{1,0:T(8,128)S(1)} %get-tuple-element.166, f32[64,128]{1,0:T(8,128)S(1)} %get-tuple-element.167, f32[64,128]{1,0:T(8,128)S(1)} %get-tuple-element.168, ...), kind=kLoop, calls=%fused_computation.150 | loop fusion | flops 54476800 | bytes 688128 | tf_op jit(solution)/shard_map/while/body/eval_jaxpr/reduce_sum | solution.py:73
  119.2 3.4 collective-permute-start.8
  130.0 25.7 %all-gather.2 = bf16[16,3,441]{2,1,0:T(4,128)(2,1)S(1)} all-gather(bf16[1,3,441]{2,1,0:T(4,128)(2,1)S(1)} %fusion.266), channel_id=2, replica_groups=mesh['sector'=16,'box'=16] {'sector'}, dimensions={0}, use_global_device_ids=true | all-gather | bytes 44982 | tf_op jit(solution)/shard_map/all_gather | solution.py:157
  155.7 4.6 %fusion.262 = f32[3,441]{1,0:T(4,128)S(1)} fusion(bf16[16,441,441]{2,1,0:T(8,128)(2,1)} %gather_fusion.3, bf16[1,441,441]{2,0,1:T(2,128)(2,1)} %get-tuple-element.125, bf16[16,3,441]{2,1,0:T(4,128)(2,1)S(1)} %all-gather.2, pred[16]{0:T(512)(128)(4,1)} %fusion.434), kind=kOutput, calls=%fused_computation.344 | convolution fusion | flops 19859554 | bytes 6659998 | tf_op jit(solution)/shard_map/cy,xy->cx/dot_general | solution.py:167
  171.9 2.6 fusion.173
  175.6 3.3 reshape.4930
  179.0 6.0 %fusion.131 = f32[3,64,128]{2,0,1:T(4,128)S(1)} fusion(f32[64,3,21,21]{3,2,1,0:T(8,128)} %reshape.4930, f32[21,64,128]{2,0,1:T(8,128)} %copy.323, f32[21,64,128,1]{2,1,0,3:T(8,128)S(1)} %bitcast.1390), kind=kOutput, calls=%fused_computation.240 | convolution fusion | flops 131063808 | bytes 1813248 | tf_op jit(solution)/shard_map/ncjk,knp->cjnp/dot_general | solution.py:60
  186.3 29.1 %fusion.69 = (f32[64,128]{1,0:T(8,128)S(1)}, f32[64,128]{1,0:T(8,128)S(1)}, f32[64,128]{1,0:T(8,128)S(1)}, f32[64,128]{1,0:T(8,128)S(1)}, f32[64,128]{1,0:T(8,12...) fusion(f32[64,128]{1,0:T(8,128)S(1)} %get-tuple-element.142, ...), kind=kLoop, calls=%fused_computation.174 | loop fusion | flops 81715200 | bytes 884736 | tf_op jit(solution)/shard_map/while/body/eval_jaxpr/reduce_sum | solution.py:73
  219.6 5.5 %fusion.132 = f32[64,3,21,21]{3,2,1,0:T(8,128)} fusion(f32[21,64,128]{2,0,1:T(8,128)S(1)} %copy.364, f32[3,64,128]{2,0,1:T(4,128)S(1)} %copy-done.14, f32[21,64,128,1]{2,1,0,3:T(8,128)S(1)} %bitcast.1387), kind=kOutput, calls=%fused_computation.241 | convolution fusion | flops 130572288 | bytes 1813248 | tf_op jit(solution)/shard_map/cjnp,knp->ncjk/dot_general | solution.py:55
  225.2 3.3 copy.366
  244.7 2.6 copy.381
  248.6 3.0 collective-permute-start.9
  260.8 4.5 %collective-permute-start.16 = (bf16[3,441]{1,0:T(4,128)(2,1)S(1)}, bf16[3,441]{1,0:T(4,128)(2,1)S(1)}, u32[]{:S(2)}, u32[]{:S(2)}) collective-permute-start(bf16[3,441]{1,0:T(4,128)(2,1)S(1)} %fusion.249), channel_id=1, source_target_pairs={{0,8},{8,0},{1,9},{9,1},{2,10},{10,2},{3,11},{11,3},{4,12},{12,4},... | collective-permute-start | bytes 7946 | tf_op jit(solution)/shard_map/ppermute | solution.py:37
  265.3 24.4 %fusion.105 = (f32[64,128]{1,0:T(8,128)S(1)}, f32[64,128]{1,0:T(8,128)S(1)}, f32[64,128]{1,0:T(8,128)S(1)}, f32[64,128]{1,0:T(8,128)S(1)}, f32[64,128]{1,0:T(8,128)S(1)}, /*index=5*/f32[64,128]{1,0:T(8,128)}) fusion(f32[64,128]{1,0:T(8,128)S(1)} %get-tuple-element.154, f32[64,128]{1,0:T(8,128)S(1)} %get-tuple-element.155, ...), kind=kLoop, calls=%fused_computation.210 | loop fusion | flops 54476800 | bytes 688128 | tf_op jit(solution)/shard_map/while/body/eval_jaxpr/reduce_sum | solution.py:73
  290.0 25.9 %all-gather.3 = bf16[16,3,441]{2,1,0:T(4,128)(2,1)S(1)} all-gather(bf16[1,3,441]{2,1,0:T(4,128)(2,1)S(1)} %fusion.264), channel_id=3, replica_groups=mesh['sector'=16,'box'=16] {'sector'}, dimensions={0}, use_global_device_ids=true | all-gather | bytes 44982 | tf_op jit(solution)/shard_map/all_gather | solution.py:157
  315.9 4.6 %fusion.261 = f32[3,441]{1,0:T(4,128)S(1)} fusion(bf16[16,441,441]{2,1,0:T(8,128)(2,1)} %gather_fusion.3, bf16[1,441,441]{2,0,1:T(2,128)(2,1)} %get-tuple-element.125, bf16[16,3,441]{2,1,0:T(4,128)(2,1)S(1)} %all-gather.3, pred[16]{0:T(512)(128)(4,1)S(1)} %copy-done.61), kind=kOutput, calls=%fused_computation.343 | convolution fusion | flops 19859554 | bytes 6659998 | tf_op jit(solution)/shard_map/cy,xy->cx/dot_general | solution.py:167
  329.3 2.7 fusion.170
  335.7 5.2 %fusion.130 = f32[3,64,128]{2,0,1:T(4,128)S(1)} fusion(f32[64,3,21,21]{3,2,1,0:T(8,128)S(1)} %reshape.4932, f32[21,64,128]{2,0,1:T(8,128)S(1)} %copy-done.5, f32[21,64,128,1]{2,1,0,3:T(8,128)} %bitcast.1388), kind=kOutput, calls=%fused_computation.238 | convolution fusion | flops 131063808 | bytes 1813248 | tf_op jit(solution)/shard_map/ncjk,knp->cjnp/dot_general | solution.py:60
  342.1 28.9 %fusion.129 = (f32[64,128]{1,0:T(8,128)S(1)}, f32[64,128]{1,0:T(8,128)S(1)}, f32[64,128]{1,0:T(8,128)S(1)}, f32[64,128]{1,0:T(8,128)S(1)}, f32[64,128]{1,0:T(8,1...) fusion(f32[64,128]{1,0:T(8,128)S(1)} %get-tuple-element.130, ...), kind=kLoop, calls=%fused_computation.234 | loop fusion | flops 81715200 | bytes 884736 | tf_op jit(solution)/shard_map/while/body/eval_jaxpr/reduce_sum | solution.py:73
  (377 shorter events, 105.9 us)
Async XLA Ops:
  6.7 178.3 %collective-permute-start.3 = (bf16[6,1,64,128]{3,2,1,0:T(8,128)(2,1)}, bf16[6,1,64,128]{3,2,1,0:T(8,128)(2,1)}, u32[]{:S(2)}, u32[]{:S(2)}) collective-permute-start(bf16[6,1,64,128]{3,2,1,0:T(8,128)(2,1)} %get-tuple-element.196), channel_id=1, source_target_pairs={{16,0},{32,16},{48,32},{64,48},{80,64},{96,80},{112,96},{128,112},... | collective-permute-start | bytes 294920 | tf_op jit(solution)/shard_map/ppermute | solution.py:25
  9.0 176.0 %collective-permute-start.2 = (bf16[6,1,64,128]{3,2,1,0:T(8,128)(2,1)}, bf16[6,1,64,128]{3,2,1,0:T(8,128)(2,1)}, u32[]{:S(2)}, u32[]{:S(2)}) collective-permute-start(bf16[6,1,64,128]{3,2,1,0:T(8,128)(2,1)} %get-tuple-element.196), channel_id=1, source_target_pairs={{0,16},{16,32},{32,48},{48,64},{64,80},{80,96},{96,112},{112,128},... | collective-permute-start | bytes 294920 | tf_op jit(solution)/shard_map/ppermute | solution.py:24
  15.2 21.2 %copy-start.2 = (bf16[2,441,441]{2,0,1:T(2,128)(2,1)S(1)}, bf16[2,441,441]{2,0,1:T(2,128)(2,1)}, u32[]{:S(2)}) copy-start(bf16[2,441,441]{2,0,1:T(2,128)(2,1)} %param.21) | copy-start | bytes 2333776
  23.1 42.2 %collective-permute-start.4 = (f32[6,256]{1,0:T(8,128)S(1)}, f32[6,256]{1,0:T(8,128)S(1)}, u32[]{:S(2)}, u32[]{:S(2)}) collective-permute-start(f32[6,256]{1,0:T(8,128)S(1)} %pad_maximum_fusion.6), channel_id=1, source_target_pairs={{0,16},{16,32},{32,48},{48,64},{64,80},{80,96},{96,112},{112,128},... | collective-permute-start | bytes 18440 | tf_op jit(solution)/shard_map/ppermute | solution.py:42
  25.0 57.4 %collective-permute-start.1 = (bf16[6,1,1,128]{3,2,0,1:T(2,128)(2,1)}, bf16[6,1,1,128]{3,2,0,1:T(2,128)(2,1)}, u32[]{:S(2)}, u32[]{:S(2)}) collective-permute-start(bf16[6,1,1,128]{3,2,0,1:T(2,128)(2,1)} %get-tuple-element.192), channel_id=1, source_target_pairs={{1,0},{2,1},{3,2},{4,3},{5,4},{6,5},{7,6},{8,7},{9,8},{10,9},{11,1... | collective-permute-start | bytes 4616 | tf_op jit(solution)/shard_map/ppermute | solution.py:25
  26.3 56.1 %collective-permute-start = (bf16[6,1,1,128]{3,2,0,1:T(2,128)(2,1)}, bf16[6,1,1,128]{3,2,0,1:T(2,128)(2,1)}, u32[]{:S(2)}, u32[]{:S(2)}) collective-permute-start(bf16[6,1,1,128]{3,2,0,1:T(2,128)(2,1)} %get-tuple-element.191), channel_id=1, source_target_pairs={{0,1},{1,2},{2,3},{3,4},{4,5},{5,6},{6,7},{7,8},{8,9},{9,10},{10,1... | collective-permute-start | bytes 4616 | tf_op jit(solution)/shard_map/ppermute | solution.py:24
  81.4 1.8 collective-permute-start.5
  83.6 3.6 collective-permute-start.6
  87.5 30.8 %collective-permute-start.7 = (bf16[3,441]{1,0:T(4,128)(2,1)S(1)}, bf16[3,441]{1,0:T(4,128)(2,1)S(1)}, u32[]{:S(2)}, u32[]{:S(2)}) collective-permute-start(bf16[3,441]{1,0:T(4,128)(2,1)S(1)} %fusion.240), channel_id=1, source_target_pairs={{0,4},{4,0},{1,5},{5,1},{2,6},{6,2},{3,7},{7,3},{8,12},{12,8},{9,1... | collective-permute-start | bytes 7946 | tf_op jit(solution)/shard_map/ppermute | solution.py:37
  119.2 9.1 %collective-permute-start.8 = (bf16[3,441]{1,0:T(4,128)(2,1)}, bf16[3,441]{1,0:T(4,128)(2,1)}, u32[]{:S(2)}, u32[]{:S(2)}) collective-permute-start(bf16[3,441]{1,0:T(4,128)(2,1)} %fusion.241), channel_id=1, source_target_pairs={{0,8},{8,0},{1,9},{9,1},{2,10},{10,2},{3,11},{11,3},{4,12},{12,4},... | collective-permute-start | bytes 7946 | tf_op jit(solution)/shard_map/ppermute | solution.py:37
  184.9 31.4 %copy-start.15 = (f32[3,64,128]{2,0,1:T(4,128)}, f32[3,64,128]{2,0,1:T(4,128)S(1)}, u32[]{:S(2)}) copy-start(f32[3,64,128]{2,0,1:T(4,128)S(1)} %fusion.131) | copy-start | bytes 294916
  184.9 30.6 %copy-start.26 = (f32[64,128]{1,0:T(8,128)S(1)}, f32[64,128]{1,0:T(8,128)}, u32[]{:S(2)}) copy-start(f32[64,128]{1,0:T(8,128)} %get-tuple-element.80) | copy-start | bytes 98308
  185.0 30.6 %copy-start.27 = (f32[64,128]{1,0:T(8,128)S(1)}, f32[64,128]{1,0:T(8,128)}, u32[]{:S(2)}) copy-start(f32[64,128]{1,0:T(8,128)} %get-tuple-element.81) | copy-start | bytes 98308
  185.0 30.6 %copy-start.28 = (f32[64,128]{1,0:T(8,128)S(1)}, f32[64,128]{1,0:T(8,128)}, u32[]{:S(2)}) copy-start(f32[64,128]{1,0:T(8,128)} %get-tuple-element.82) | copy-start | bytes 98308
  185.0 30.6 %copy-start.29 = (f32[64,128]{1,0:T(8,128)S(1)}, f32[64,128]{1,0:T(8,128)}, u32[]{:S(2)}) copy-start(f32[64,128]{1,0:T(8,128)} %get-tuple-element.107) | copy-start | bytes 98308
  185.0 30.6 %copy-start.30 = (f32[64,128]{1,0:T(8,128)S(1)}, f32[64,128]{1,0:T(8,128)}, u32[]{:S(2)}) copy-start(f32[64,128]{1,0:T(8,128)} %get-tuple-element.108) | copy-start | bytes 98308
  185.0 30.6 %copy-start.31 = (f32[64,128]{1,0:T(8,128)S(1)}, f32[64,128]{1,0:T(8,128)}, u32[]{:S(2)}) copy-start(f32[64,128]{1,0:T(8,128)} %get-tuple-element.109) | copy-start | bytes 98308
  185.0 31.3 %copy-start.6 = (f32[21,64,128]{2,1,0:T(8,128)S(1)}, f32[21,64,128]{2,1,0:T(8,128)}, u32[]{:S(2)}) copy-start(f32[21,64,128]{2,1,0:T(8,128)} %get-tuple-element.217) | copy-start | bytes 2064388
  185.0 31.3 %copy-start.20 = (f32[21,64,128]{2,1,0:T(8,128)S(1)}, f32[21,64,128]{2,1,0:T(8,128)}, u32[]{:S(2)}) copy-start(f32[21,64,128]{2,1,0:T(8,128)} %get-tuple-element.218) | copy-start | bytes 2064388
  186.3 33.3 %copy-start.14 = (f32[3,64,128]{2,0,1:T(4,128)S(1)}, f32[3,64,128]{2,0,1:T(4,128)}, u32[]{:S(2)}) copy-start(f32[3,64,128]{2,0,1:T(4,128)} %copy.322) | copy-start | bytes 294916
  234.7 106.2 %collective-permute-start.12 = (bf16[6,1,64,128]{3,2,1,0:T(8,128)(2,1)}, bf16[6,1,64,128]{3,2,1,0:T(8,128)(2,1)}, u32[]{:S(2)}, u32[]{:S(2)}) collective-permute-start(bf16[6,1,64,128]{3,2,1,0:T(8,128)(2,1)} %pad_maximum_fusion.2), channel_id=1, source_target_pairs={{16,0},{32,16},{48,32},{64,48},{80,64},{96,80},{112,96},{128,112},... | collective-permute-start | bytes 294920 | tf_op jit(solution)/shard_map/ppermute | solution.py:25
  236.7 104.2 %collective-permute-start.11 = (bf16[6,1,64,128]{3,2,1,0:T(8,128)(2,1)}, bf16[6,1,64,128]{3,2,1,0:T(8,128)(2,1)}, u32[]{:S(2)}, u32[]{:S(2)}) collective-permute-start(bf16[6,1,64,128]{3,2,1,0:T(8,128)(2,1)} %pad_maximum_fusion.2), channel_id=1, source_target_pairs={{0,16},{16,32},{32,48},{48,64},{64,80},{80,96},{96,112},{112,128},... | collective-permute-start | bytes 294920 | tf_op jit(solution)/shard_map/ppermute | solution.py:24
  241.4 10.3 %collective-permute-start.13 = (bf16[3,441]{1,0:T(4,128)(2,1)S(1)}, bf16[3,441]{1,0:T(4,128)(2,1)S(1)}, u32[]{:S(2)}, u32[]{:S(2)}) collective-permute-start(bf16[3,441]{1,0:T(4,128)(2,1)S(1)} %fusion.236), channel_id=1, source_target_pairs={{0,1},{1,0},{2,3},{3,2},{4,5},{5,4},{6,7},{7,6},{8,9},{9,8},{10,11... | collective-permute-start | bytes 7946 | tf_op jit(solution)/shard_map/ppermute | solution.py:37
  244.7 20.7 %copy-start.55 = (f32[64,128]{1,0:T(8,128)S(1)}, f32[64,128]{1,0:T(8,128)}, u32[]{:S(2)}) copy-start(f32[64,128]{1,0:T(8,128)} %get-tuple-element.184) | copy-start | bytes 98308
  247.3 6.4 %collective-permute-start.10 = (bf16[6,1,1,128]{3,2,1,0:T(2,128)(2,1)}, bf16[6,1,1,128]{3,2,1,0:T(2,128)(2,1)S(1)}, u32[]{:S(2)}, u32[]{:S(2)}) collective-permute-start(bf16[6,1,1,128]{3,2,1,0:T(2,128)(2,1)} %get-tuple-element.179), channel_id=1, source_target_pairs={{1,0},{2,1},{3,2},{4,3},{5,4},{6,5},{7,6},{8,7},{9,8},{10,9},{11,1... | collective-permute-start | bytes 4616 | tf_op jit(solution)/shard_map/ppermute | solution.py:25
  248.6 5.0 %collective-permute-start.9 = (bf16[6,1,1,128]{3,2,1,0:T(2,128)(2,1)S(1)}, bf16[6,1,1,128]{3,2,1,0:T(2,128)(2,1)S(1)}, u32[]{:S(2)}, u32[]{:S(2)}) collective-permute-start(bf16[6,1,1,128]{3,2,1,0:T(2,128)(2,1)S(1)} %get-tuple-element.178), channel_id=1, source_target_pairs={{0,1},{1,2},{2,3},{3,4},{4,5},{5,6},{6,7},{7,8},{8,9},{9,10},{10,1... | collective-permute-start | bytes 4616 | tf_op jit(solution)/shard_map/ppermute | solution.py:24
  251.8 64.1 %copy-start.61 = (pred[16]{0:T(512)(128)(4,1)S(1)}, pred[16]{0:T(512)(128)(4,1)}, u32[]{:S(2)}) copy-start(pred[16]{0:T(512)(128)(4,1)} %fusion.434) | copy-start | bytes 52
  252.0 3.6 collective-permute-start.14
  256.0 4.5 %collective-permute-start.15 = (bf16[3,441]{1,0:T(4,128)(2,1)S(1)}, bf16[3,441]{1,0:T(4,128)(2,1)S(1)}, u32[]{:S(2)}, u32[]{:S(2)}) collective-permute-start(bf16[3,441]{1,0:T(4,128)(2,1)S(1)} %fusion.248), channel_id=1, source_target_pairs={{0,4},{4,0},{1,5},{5,1},{2,6},{6,2},{3,7},{7,3},{8,12},{12,8},{9,1... | collective-permute-start | bytes 7946 | tf_op jit(solution)/shard_map/ppermute | solution.py:37
  260.8 28.9 %collective-permute-start.16 = (bf16[3,441]{1,0:T(4,128)(2,1)S(1)}, bf16[3,441]{1,0:T(4,128)(2,1)S(1)}, u32[]{:S(2)}, u32[]{:S(2)}) collective-permute-start(bf16[3,441]{1,0:T(4,128)(2,1)S(1)} %fusion.249), channel_id=1, source_target_pairs={{0,8},{8,0},{1,9},{9,1},{2,10},{10,2},{3,11},{11,3},{4,12},{12,4},... | collective-permute-start | bytes 7946 | tf_op jit(solution)/shard_map/ppermute | solution.py:37
  340.9 30.0 %copy-start.24 = (f32[3,1,64,128]{3,2,1,0:T(8,128)S(1)}, f32[3,1,64,128]{3,2,1,0:T(8,128)}, u32[]{:S(2)}) copy-start(f32[3,1,64,128]{3,2,1,0:T(8,128)} %get-tuple-element.115) | copy-start | bytes 294916
  340.9 30.0 %copy-start.41 = (f32[64,128]{1,0:T(8,128)S(1)}, f32[64,128]{1,0:T(8,128)}, u32[]{:S(2)}) copy-start(f32[64,128]{1,0:T(8,128)} %get-tuple-element.100) | copy-start | bytes 98308
  (48 other events, 405.8 us)
where the time goes:
time: 379 us; the launch traced here: 372 us
  other arithmetic  128 us (34%)
  local copies, waits for them, and re-layouts  80.1 us (21%)
  matrix products  69.6 us (18%)
  blocking collectives  51.6 us (14%)
  starting transfers between devices  34.2 us (9%)
  waiting for transfers between devices  5.86 us (2%)
    reduce_sum x4, other arithmetic, pair_velocity(): jnp.sum(inverse * (weight_y * delta_z - weight_z * delta_y), axis=2)  108 us
    all_gather x2, blocking collectives, far_field(): piece = lax.all_gather(current[None], 'sector', axis=0, tiled=True)  51.6 us
    dot_general x8, matrix products, far_field(): jnp.einsum('cy,xy->cx', local, up_side, preferred_element_type=jnp.float32)  19.6 us
    ppermute x8, starting transfers between devices, partner_2(): return lax.ppermute(block, axis, route)  19.3 us
    dot_general x2, matrix products, evaluate(): jnp.einsum('ncjk,knp->cjnp', shaped, cheb_b, precision=HIGHEST_PRECISION)  11.1 us
    dot_general x2, matrix products, multipoles(): jnp.einsum('cjnp,knp->ncjk', weighted, cheb_b, precision=HIGHEST_PRECISION)  10.9 us
    convert_element_type x6, local copies, waits for them, and re-layouts, far_field(): leaf = (multipoles(cheb_a, cheb_b, weights) + arrival_terms).reshape(box_...  10 us
    reshape x4, local copies, waits for them, and re-layouts, far_field(): presum = presum.astype(jnp.bfloat16).reshape(NCLASS, box_count * 3, coef)  8.64 us
  transfers between devices with their start and end apart: 17, of which 4 were waited for; matrix products, arithmetic and copies ran while one was open for 52% of the time, Pallas kernels for 0%

commit v1 on v0

--- a/solution.py
+++ b/solution.py
@@ -154,7 +154,14 @@
         current = merge_pair(current, partner, side_bit, tree_up)
     sector_index = lax.axis_index("sector")
     sector_count = lax.axis_size("sector")
-    piece = lax.all_gather(current[None], "sector", axis=0, tiled=True)
+    ring = [current[None]]
+    for hop in range(15):
+        ring.append(lax.ppermute(ring[-1], "sector", [(dev, (dev + 1) % 16) for dev in range(16)]))
+    piece = jnp.roll(
+        jnp.concatenate(ring[::-1], axis=0),
+        (lax.axis_index("sector") + 1) * ring[0].shape[0],
+        axis=0,
+    )
     source_ids = jnp.arange(piece.shape[0], dtype=jnp.int32)
     distance = (source_ids - sector_index) % sector_count
     matrices = m2l_sector[jnp.maximum(distance - 1, 0)]

time: 379 us -> 518 us (1.37)
  the two profiles are of different devices: /device:TPU:2 before, /device:TPU:30 now
where the time goes in v1:
time: 518 us; the launch traced here: 509 us
  starting transfers between devices  152 us (29%)
  other arithmetic  127 us (25%)
  local copies, waits for them, and re-layouts  105 us (20%)
  matrix products  75.1 us (14%)
  waiting for transfers between devices  46.9 us (9%)
    ppermute x30, starting transfers between devices, far_field(): lax.ppermute(ring[-1], 'sector', [(dev, (dev + 1) % 16) for dev in range(...  118 us
    reduce_sum x4, other arithmetic, pair_velocity(): jnp.sum(inverse * (weight_y * delta_z - weight_z * delta_y), axis=2)  109 us
    ppermute x30, waiting for transfers between devices, far_field(): lax.ppermute(ring[-1], 'sector', [(dev, (dev + 1) % 16) for dev in range(...  28.6 us
    unnamed x186, local copies, waits for them, and re-layouts  27.1 us
    dot_general x8, matrix products, far_field(): jnp.einsum('cy,xy->cx', local, up_side, preferred_element_type=jnp.float32)  22.1 us
    ppermute x8, waiting for transfers between devices, partner_2(): return lax.ppermute(block, axis, route)  18.3 us
    ppermute x4, starting transfers between devices, with_halo(): before = lax.ppermute(last, axis, up)  15.8 us
    ppermute x8, starting transfers between devices, partner_2(): return lax.ppermute(block, axis, route)  12.3 us
  transfers between devices with their start and end apart: 47, of which 26 were waited for; matrix products, arithmetic and copies ran while one was open for 38% of the time, Pallas kernels for 0%

profile of v1, /device:TPU:30, one launch (start us, length us, event | category | flops | bytes accessed | tf_op | source)
XLA Modules:
  0.0 508.8 jit_solution(11413444478604988614)
XLA Ops:
  20.8 5.4 %fusion.134 = f32[64,3,21,21]{3,2,1,0:T(8,128)} fusion(f32[21,64,128]{2,0,1:T(8,128)S(1)} %copy.323, f32[3,64,128]{2,0,1:T(4,128)S(1)} %copy.322, f32[21,64,128,1]{2,1,0,3:T(8,128)S(1)} %bitcast.1389), kind=kOutput, calls=%fused_computation.243 | convolution fusion | flops 130572288 | bytes 1813248 | tf_op jit(solution)/shard_map/cjnp,knp->ncjk/dot_general | solution.py:55
  26.2 6.4 %constant_dynamic-slice_fusion.1 = (bf16[1,441,441]{2,0,1:T(2,128)(2,1)}, bf16[1,441,441]{2,0,1:T(2,128)(2,1)}, bf16[1,441,441]{2,0,1:T(2,128)(2,1)}, bf16[1,441...) fusion(bf16[2,441,441]{2,0,1:T(2,128)(2,1)S(1)} %copy-done.2, s32[]{:T(128)S(6)} %select_n.171, ...), kind=kLoop, calls=%fused_computation.848 | loop fusion | bytes 4667560 | tf_op jit(solution)/shard_map/jit(dynamic_index_in_dim)/dynamic_slice | solution.py:172
  58.3 5.5 %collective-permute-start.8 = (bf16[3,441]{1,0:T(4,128)(2,1)S(1)}, bf16[3,441]{1,0:T(4,128)(2,1)S(1)}, u32[]{:S(2)}, u32[]{:S(2)}) collective-permute-start(bf16[3,441]{1,0:T(4,128)(2,1)S(1)} %fusion.241), channel_id=1, source_target_pairs={{0,8},{8,0},{1,9},{9,1},{2,10},{10,2},{3,11},{11,3},{4,12},{12,4},... | collective-permute-start | bytes 7946 | tf_op jit(solution)/shard_map/ppermute | solution.py:37
  78.4 6.7 %constant_dynamic-slice_fusion = (bf16[1,441,441]{2,0,1:T(2,128)(2,1)}, bf16[1,441,441]{2,0,1:T(2,128)(2,1)}, bf16[1,441,441]{2,0,1:T(2,128)(2,1)}, bf16[1,441,441]{2,0,1:T(2,128)(2,1)}) fusion(bf16[2,441,441]{2,0,1:T(2,128)(2,1)} %param.24, s32[]{:T(128)S(6)} %select_n.171, s32[]{:T(128)S(6)} %select_n.170, s32[]{:T(128)S(6)} %select_n.169, s32[]{:T(128)S(6)} %select_n.168), kind=kLoop, calls=%fused_computation.847 | loop fusion | bytes 3111712 | tf_op jit(solution)/shard_map/jit(dynamic_index_in_dim)/dynamic_slice | solution.py:173
  93.6 5.6 %collective-permute-start.13 = (bf16[1,3,441]{2,1,0:T(4,128)(2,1)S(1)}, bf16[1,3,441]{2,1,0:T(4,128)(2,1)S(1)}, u32[]{:S(2)}, u32[]{:S(2)}) collective-permute-start(bf16[1,3,441]{2,1,0:T(4,128)(2,1)S(1)} %collective-permute-done.12), channel_id=1, source_target_pairs={{0,16},{16,32},{32,48},{48,64},{64,80},{80,96},{96,112},{112,128},... | collective-permute-start | bytes 7946 | tf_op jit(solution)/shard_map/ppermute | solution.py:159
  100.6 5.6 %collective-permute-start.14 = (bf16[1,3,441]{2,1,0:T(4,128)(2,1)S(1)}, bf16[1,3,441]{2,1,0:T(4,128)(2,1)S(1)}, u32[]{:S(2)}, u32[]{:S(2)}) collective-permute-start(bf16[1,3,441]{2,1,0:T(4,128)(2,1)S(1)} %collective-permute-done.13), channel_id=1, source_target_pairs={{0,16},{16,32},{32,48},{48,64},{64,80},{80,96},{96,112},{112,128},... | collective-permute-start | bytes 7946 | tf_op jit(solution)/shard_map/ppermute | solution.py:159
  107.5 5.6 %collective-permute-start.15 = (bf16[1,3,441]{2,1,0:T(4,128)(2,1)S(1)}, bf16[1,3,441]{2,1,0:T(4,128)(2,1)S(1)}, u32[]{:S(2)}, u32[]{:S(2)}) collective-permute-start(bf16[1,3,441]{2,1,0:T(4,128)(2,1)S(1)} %collective-permute-done.14), channel_id=1, source_target_pairs={{0,16},{16,32},{32,48},{48,64},{64,80},{80,96},{96,112},{112,128},... | collective-permute-start | bytes 7946 | tf_op jit(solution)/shard_map/ppermute | solution.py:159
  114.5 5.7 %collective-permute-start.16 = (bf16[1,3,441]{2,1,0:T(4,128)(2,1)S(1)}, bf16[1,3,441]{2,1,0:T(4,128)(2,1)S(1)}, u32[]{:S(2)}, u32[]{:S(2)}) collective-permute-start(bf16[1,3,441]{2,1,0:T(4,128)(2,1)S(1)} %collective-permute-done.15), channel_id=1, source_target_pairs={{0,16},{16,32},{32,48},{48,64},{64,80},{80,96},{96,112},{112,128},... | collective-permute-start | bytes 7946 | tf_op jit(solution)/shard_map/ppermute | solution.py:159
  121.5 5.6 %collective-permute-start.17 = (bf16[1,3,441]{2,1,0:T(4,128)(2,1)S(1)}, bf16[1,3,441]{2,1,0:T(4,128)(2,1)S(1)}, u32[]{:S(2)}, u32[]{:S(2)}) collective-permute-start(bf16[1,3,441]{2,1,0:T(4,128)(2,1)S(1)} %collective-permute-done.16), channel_id=1, source_target_pairs={{0,16},{16,32},{32,48},{48,64},{64,80},{80,96},{96,112},{112,128},... | collective-permute-start | bytes 7946 | tf_op jit(solution)/shard_map/ppermute | solution.py:159
  128.4 5.6 %collective-permute-start.18 = (bf16[1,3,441]{2,1,0:T(4,128)(2,1)S(1)}, bf16[1,3,441]{2,1,0:T(4,128)(2,1)S(1)}, u32[]{:S(2)}, u32[]{:S(2)}) collective-permute-start(bf16[1,3,441]{2,1,0:T(4,128)(2,1)S(1)} %collective-permute-done.17), channel_id=1, source_target_pairs={{0,16},{16,32},{32,48},{48,64},{64,80},{80,96},{96,112},{112,128},... | collective-permute-start | bytes 7946 | tf_op jit(solution)/shard_map/ppermute | solution.py:159
  135.3 5.6 %collective-permute-start.19 = (bf16[1,3,441]{2,1,0:T(4,128)(2,1)S(1)}, bf16[1,3,441]{2,1,0:T(4,128)(2,1)S(1)}, u32[]{:S(2)}, u32[]{:S(2)}) collective-permute-start(bf16[1,3,441]{2,1,0:T(4,128)(2,1)S(1)} %collective-permute-done.18), channel_id=1, source_target_pairs={{0,16},{16,32},{32,48},{48,64},{64,80},{80,96},{96,112},{112,128},... | collective-permute-start | bytes 7946 | tf_op jit(solution)/shard_map/ppermute | solution.py:159
  141.5 6.9 %gather_fusion.3 = bf16[16,441,441]{2,1,0:T(8,128)(2,1)} fusion(bf16[15,441,441]{2,1,0:T(8,128)(2,1)} %param.25, s32[1024]{0:T(1024)S(1)} %pad_clamp_fusion), kind=kCustom, calls=%fused_computation.3 | custom fusion | bytes 12446848 | tf_op jit(solution)/shard_map/gather | solution.py:167
  156.9 5.7 %collective-permute-start.22 = (bf16[1,3,441]{2,1,0:T(4,128)(2,1)}, bf16[1,3,441]{2,1,0:T(4,128)(2,1)}, u32[]{:S(2)}, u32[]{:S(2)}) collective-permute-start(bf16[1,3,441]{2,1,0:T(4,128)(2,1)} %collective-permute-done.21), channel_id=1, source_target_pairs={{0,16},{16,32},{32,48},{48,64},{64,80},{80,96},{96,112},{112,128},... | collective-permute-start | bytes 7946 | tf_op jit(solution)/shard_map/ppermute | solution.py:159
  162.6 25.5 %fusion.45 = (f32[64,128]{1,0:T(8,128)S(1)}, f32[64,128]{1,0:T(8,128)}, f32[64,128]{1,0:T(8,128)}, f32[64,128]{1,0:T(8,128)}, f32[64,128]{1,0:T(8,128)}, /*index=5*/f32[64,128]{1,0:T(8,128)}) fusion(f32[64,128]{1,0:T(8,128)S(1)} %get-tuple-element.167, f32[64,128]{1,0:T(8,128)S(1)} %get-tuple-element.168, f32[64,128]{1,0:T(8,128)S(1)} %get-tuple-element.169, ...), kind=kLoop, calls=%fused_computation.150 | loop fusion | flops 54476800 | bytes 688128 | tf_op jit(solution)/shard_map/while/body/eval_jaxpr/reduce_sum | solution.py:73
  218.2 5.2 %fusion.262 = f32[3,441]{1,0:T(4,128)} fusion(bf16[16,441,441]{2,1,0:T(8,128)(2,1)} %gather_fusion.3, bf16[1,441,441]{2,0,1:T(2,128)(2,1)} %get-tuple-element.126, s32[]{:T(128)S(6)} %select_n.184, bf16[16,3,441]{2,1,0:T(4,128)(2,1)} %constant_dynamic-update-slice_fusion.84, pred[16]{0:T(512)(128)(4,1)} %fusion.442), kind=kOutput, calls=%fused_computation.344 | convolution fusion | flops 19944226 | bytes 6660002 | tf_op jit(solution)/shard_map/cy,xy->cx/dot_general | solution.py:174
  248.2 6.1 %fusion.131 = f32[3,64,128]{2,0,1:T(4,128)S(1)} fusion(f32[64,3,21,21]{3,2,1,0:T(8,128)} %reshape.4922, f32[21,64,128]{2,0,1:T(8,128)} %copy-done.3, f32[21,64,128,1]{2,1,0,3:T(8,128)} %bitcast.1390), kind=kOutput, calls=%fused_computation.240 | convolution fusion | flops 131063808 | bytes 1813248 | tf_op jit(solution)/shard_map/ncjk,knp->cjnp/dot_general | solution.py:60
  255.6 29.3 %fusion.69 = (f32[64,128]{1,0:T(8,128)S(1)}, f32[64,128]{1,0:T(8,128)S(1)}, f32[64,128]{1,0:T(8,128)S(1)}, f32[64,128]{1,0:T(8,128)S(1)}, f32[64,128]{1,0:T(8,12...) fusion(f32[64,128]{1,0:T(8,128)S(1)} %get-tuple-element.143, ...), kind=kLoop, calls=%fused_computation.174 | loop fusion | flops 81715200 | bytes 884736 | tf_op jit(solution)/shard_map/while/body/eval_jaxpr/reduce_sum | solution.py:73
  289.0 5.5 %fusion.132 = f32[64,3,21,21]{3,2,1,0:T(8,128)} fusion(f32[21,64,128]{2,0,1:T(8,128)S(1)} %copy.364, f32[3,64,128]{2,0,1:T(4,128)S(1)} %copy-done.12, f32[21,64,128,1]{2,1,0,3:T(8,128)S(1)} %bitcast.1387), kind=kOutput, calls=%fused_computation.241 | convolution fusion | flops 130572288 | bytes 1813248 | tf_op jit(solution)/shard_map/cjnp,knp->ncjk/dot_general | solution.py:55
  322.5 5.1 %collective-permute-done.31 = bf16[3,441]{1,0:T(4,128)(2,1)S(1)} collective-permute-done((bf16[3,441]{1,0:T(4,128)(2,1)S(1)}, bf16[3,441]{1,0:T(4,128)(2,1)S(1)}, u32[]{:S(2)}, u32[]{:S(2)}) %collective-permute-start.31) | collective-permute-done | bytes 2678 | tf_op jit(solution)/shard_map/ppermute | solution.py:37
  336.3 5.6 %collective-permute-start.34 = (bf16[1,3,441]{2,1,0:T(4,128)(2,1)S(1)}, bf16[1,3,441]{2,1,0:T(4,128)(2,1)S(1)}, u32[]{:S(2)}, u32[]{:S(2)}) collective-permute-start(bf16[1,3,441]{2,1,0:T(4,128)(2,1)S(1)} %collective-permute-done.33), channel_id=1, source_target_pairs={{0,16},{16,32},{32,48},{48,64},{64,80},{80,96},{96,112},{112,128},... | collective-permute-start | bytes 7946 | tf_op jit(solution)/shard_map/ppermute | solution.py:159
  343.2 5.6 %collective-permute-start.35 = (bf16[1,3,441]{2,1,0:T(4,128)(2,1)S(1)}, bf16[1,3,441]{2,1,0:T(4,128)(2,1)S(1)}, u32[]{:S(2)}, u32[]{:S(2)}) collective-permute-start(bf16[1,3,441]{2,1,0:T(4,128)(2,1)S(1)} %collective-permute-done.34), channel_id=1, source_target_pairs={{0,16},{16,32},{32,48},{48,64},{64,80},{80,96},{96,112},{112,128},... | collective-permute-start | bytes 7946 | tf_op jit(solution)/shard_map/ppermute | solution.py:159
  350.1 5.6 %collective-permute-start.36 = (bf16[1,3,441]{2,1,0:T(4,128)(2,1)S(1)}, bf16[1,3,441]{2,1,0:T(4,128)(2,1)S(1)}, u32[]{:S(2)}, u32[]{:S(2)}) collective-permute-start(bf16[1,3,441]{2,1,0:T(4,128)(2,1)S(1)} %collective-permute-done.35), channel_id=1, source_target_pairs={{0,16},{16,32},{32,48},{48,64},{64,80},{80,96},{96,112},{112,128},... | collective-permute-start | bytes 7946 | tf_op jit(solution)/shard_map/ppermute | solution.py:159
  357.1 5.6 %collective-permute-start.37 = (bf16[1,3,441]{2,1,0:T(4,128)(2,1)S(1)}, bf16[1,3,441]{2,1,0:T(4,128)(2,1)S(1)}, u32[]{:S(2)}, u32[]{:S(2)}) collective-permute-start(bf16[1,3,441]{2,1,0:T(4,128)(2,1)S(1)} %collective-permute-done.36), channel_id=1, source_target_pairs={{0,16},{16,32},{32,48},{48,64},{64,80},{80,96},{96,112},{112,128},... | collective-permute-start | bytes 7946 | tf_op jit(solution)/shard_map/ppermute | solution.py:159
  364.0 5.6 %collective-permute-start.38 = (bf16[1,3,441]{2,1,0:T(4,128)(2,1)S(1)}, bf16[1,3,441]{2,1,0:T(4,128)(2,1)S(1)}, u32[]{:S(2)}, u32[]{:S(2)}) collective-permute-start(bf16[1,3,441]{2,1,0:T(4,128)(2,1)S(1)} %collective-permute-done.37), channel_id=1, source_target_pairs={{0,16},{16,32},{32,48},{48,64},{64,80},{80,96},{96,112},{112,128},... | collective-permute-start | bytes 7946 | tf_op jit(solution)/shard_map/ppermute | solution.py:159
  370.9 5.6 %collective-permute-start.39 = (bf16[1,3,441]{2,1,0:T(4,128)(2,1)S(1)}, bf16[1,3,441]{2,1,0:T(4,128)(2,1)S(1)}, u32[]{:S(2)}, u32[]{:S(2)}) collective-permute-start(bf16[1,3,441]{2,1,0:T(4,128)(2,1)S(1)} %collective-permute-done.38), channel_id=1, source_target_pairs={{0,16},{16,32},{32,48},{48,64},{64,80},{80,96},{96,112},{112,128},... | collective-permute-start | bytes 7946 | tf_op jit(solution)/shard_map/ppermute | solution.py:159
  378.3 5.2 %collective-permute-start.40 = (bf16[1,3,441]{2,1,0:T(4,128)(2,1)S(1)}, bf16[1,3,441]{2,1,0:T(4,128)(2,1)S(1)}, u32[]{:S(2)}, u32[]{:S(2)}) collective-permute-start(bf16[1,3,441]{2,1,0:T(4,128)(2,1)S(1)} %collective-permute-done.39), channel_id=1, source_target_pairs={{0,16},{16,32},{32,48},{48,64},{64,80},{80,96},{96,112},{112,128},... | collective-permute-start | bytes 7946 | tf_op jit(solution)/shard_map/ppermute | solution.py:159
  385.3 5.3 %collective-permute-start.26 = (bf16[6,1,64,128]{3,2,1,0:T(8,128)(2,1)}, bf16[6,1,64,128]{3,2,1,0:T(8,128)(2,1)}, u32[]{:S(2)}, u32[]{:S(2)}) collective-permute-start(bf16[6,1,64,128]{3,2,1,0:T(8,128)(2,1)} %pad_maximum_fusion.2), channel_id=1, source_target_pairs={{0,16},{16,32},{32,48},{48,64},{64,80},{80,96},{96,112},{112,128},... | collective-permute-start | bytes 294920 | tf_op jit(solution)/shard_map/ppermute | solution.py:24
  414.3 5.6 %collective-permute-start.45 = (bf16[1,3,441]{2,1,0:T(4,128)(2,1)S(1)}, bf16[1,3,441]{2,1,0:T(4,128)(2,1)S(1)}, u32[]{:S(2)}, u32[]{:S(2)}) collective-permute-start(bf16[1,3,441]{2,1,0:T(4,128)(2,1)S(1)} %collective-permute-done.44), channel_id=1, source_target_pairs={{0,16},{16,32},{32,48},{48,64},{64,80},{80,96},{96,112},{112,128},... | collective-permute-start | bytes 7946 | tf_op jit(solution)/shard_map/ppermute | solution.py:159
  421.2 5.6 %collective-permute-start.46 = (bf16[1,3,441]{2,1,0:T(4,128)(2,1)S(1)}, bf16[1,3,441]{2,1,0:T(4,128)(2,1)S(1)}, u32[]{:S(2)}, u32[]{:S(2)}) collective-permute-start(bf16[1,3,441]{2,1,0:T(4,128)(2,1)S(1)} %collective-permute-done.45), channel_id=1, source_target_pairs={{0,16},{16,32},{32,48},{48,64},{64,80},{80,96},{96,112},{112,128},... | collective-permute-start | bytes 7946 | tf_op jit(solution)/shard_map/ppermute | solution.py:159
  426.8 25.6 %fusion.105 = (f32[64,128]{1,0:T(8,128)}, f32[64,128]{1,0:T(8,128)}, f32[64,128]{1,0:T(8,128)}, f32[64,128]{1,0:T(8,128)}, f32[64,128]{1,0:T(8,128)}, /*index=5*/f32[64,128]{1,0:T(8,128)}) fusion(f32[64,128]{1,0:T(8,128)S(1)} %get-tuple-element.155, f32[64,128]{1,0:T(8,128)S(1)} %get-tuple-element.156, f32[64,128]{1,0:T(8,128)S(1)} %get-tuple-element.157, ...), kind=kLoop, calls=%fused_computation.210 | loop fusion | flops 54476800 | bytes 688128 | tf_op jit(solution)/shard_map/while/body/eval_jaxpr/reduce_sum | solution.py:73
  471.8 5.7 %fusion.130 = f32[3,64,128]{2,0,1:T(4,128)S(1)} fusion(f32[64,3,21,21]{3,2,1,0:T(8,128)} %reshape.4924, f32[21,64,128]{2,0,1:T(8,128)S(1)} %copy-done.5, f32[21,64,128,1]{2,1,0,3:T(8,128)S(1)} %bitcast.1388), kind=kOutput, calls=%fused_computation.238 | convolution fusion | flops 131063808 | bytes 1813248 | tf_op jit(solution)/shard_map/ncjk,knp->cjnp/dot_general | solution.py:60
  478.8 28.9 %fusion.129 = (f32[64,128]{1,0:T(8,128)S(1)}, f32[64,128]{1,0:T(8,128)S(1)}, f32[64,128]{1,0:T(8,128)S(1)}, f32[64,128]{1,0:T(8,128)S(1)}, f32[64,128]{1,0:T(8,1...) fusion(f32[64,128]{1,0:T(8,128)S(1)} %get-tuple-element.131, ...), kind=kLoop, calls=%fused_computation.234 | loop fusion | flops 81715200 | bytes 884736 | tf_op jit(solution)/shard_map/while/body/eval_jaxpr/reduce_sum | solution.py:73
  (489 shorter events, 237.9 us)
Async XLA Ops:
  15.4 20.5 %collective-permute-start.4 = (f32[6,256]{1,0:T(8,128)S(1)}, f32[6,256]{1,0:T(8,128)S(1)}, u32[]{:S(2)}, u32[]{:S(2)}) collective-permute-start(f32[6,256]{1,0:T(8,128)S(1)} %pad_maximum_fusion.6), channel_id=1, source_target_pairs={{0,16},{16,32},{32,48},{48,64},{64,80},{80,96},{96,112},{112,128},... | collective-permute-start | bytes 18440 | tf_op jit(solution)/shard_map/ppermute | solution.py:42
  58.3 11.9 %collective-permute-start.8 = (bf16[3,441]{1,0:T(4,128)(2,1)S(1)}, bf16[3,441]{1,0:T(4,128)(2,1)S(1)}, u32[]{:S(2)}, u32[]{:S(2)}) collective-permute-start(bf16[3,441]{1,0:T(4,128)(2,1)S(1)} %fusion.241), channel_id=1, source_target_pairs={{0,8},{8,0},{1,9},{9,1},{2,10},{10,2},{3,11},{11,3},{4,12},{12,4},... | collective-permute-start | bytes 7946 | tf_op jit(solution)/shard_map/ppermute | solution.py:37
  64.4 189.9 %collective-permute-start.3 = (bf16[6,1,64,128]{3,2,1,0:T(8,128)(2,1)}, bf16[6,1,64,128]{3,2,1,0:T(8,128)(2,1)}, u32[]{:S(2)}, u32[]{:S(2)}) collective-permute-start(bf16[6,1,64,128]{3,2,1,0:T(8,128)(2,1)} %get-tuple-element.197), channel_id=1, source_target_pairs={{16,0},{32,16},{48,32},{64,48},{80,64},{96,80},{112,96},{128,112},... | collective-permute-start | bytes 294920 | tf_op jit(solution)/shard_map/ppermute | solution.py:25
  66.3 188.1 %collective-permute-start.2 = (bf16[6,1,64,128]{3,2,1,0:T(8,128)(2,1)}, bf16[6,1,64,128]{3,2,1,0:T(8,128)(2,1)}, u32[]{:S(2)}, u32[]{:S(2)}) collective-permute-start(bf16[6,1,64,128]{3,2,1,0:T(8,128)(2,1)} %get-tuple-element.197), channel_id=1, source_target_pairs={{0,16},{16,32},{32,48},{48,64},{64,80},{80,96},{96,112},{112,128},... | collective-permute-start | bytes 294920 | tf_op jit(solution)/shard_map/ppermute | solution.py:24
  71.2 77.5 %collective-permute-start.1 = (bf16[6,1,1,128]{3,2,0,1:T(2,128)(2,1)}, bf16[6,1,1,128]{3,2,0,1:T(2,128)(2,1)}, u32[]{:S(2)}, u32[]{:S(2)}) collective-permute-start(bf16[6,1,1,128]{3,2,0,1:T(2,128)(2,1)} %get-tuple-element.193), channel_id=1, source_target_pairs={{1,0},{2,1},{3,2},{4,3},{5,4},{6,5},{7,6},{8,7},{9,8},{10,9},{11,1... | collective-permute-start | bytes 4616 | tf_op jit(solution)/shard_map/ppermute | solution.py:25
  72.5 76.2 %collective-permute-start = (bf16[6,1,1,128]{3,2,0,1:T(2,128)(2,1)}, bf16[6,1,1,128]{3,2,0,1:T(2,128)(2,1)}, u32[]{:S(2)}, u32[]{:S(2)}) collective-permute-start(bf16[6,1,1,128]{3,2,0,1:T(2,128)(2,1)} %get-tuple-element.192), channel_id=1, source_target_pairs={{0,1},{1,2},{2,3},{3,4},{4,5},{5,6},{6,7},{7,8},{8,9},{9,10},{10,1... | collective-permute-start | bytes 4616 | tf_op jit(solution)/shard_map/ppermute | solution.py:24
  76.1 9.0 %collective-permute-start.10 = (bf16[1,3,441]{2,1,0:T(4,128)(2,1)S(1)}, bf16[1,3,441]{2,1,0:T(4,128)(2,1)S(1)}, u32[]{:S(2)}, u32[]{:S(2)}) collective-permute-start(bf16[1,3,441]{2,1,0:T(4,128)(2,1)S(1)} %collective-permute-done.9), channel_id=1, source_target_pairs={{0,16},{16,32},{32,48},{48,64},{64,80},{80,96},{96,112},{112,128},... | collective-permute-start | bytes 7946 | tf_op jit(solution)/shard_map/ppermute | solution.py:159
  93.6 6.9 %collective-permute-start.13 = (bf16[1,3,441]{2,1,0:T(4,128)(2,1)S(1)}, bf16[1,3,441]{2,1,0:T(4,128)(2,1)S(1)}, u32[]{:S(2)}, u32[]{:S(2)}) collective-permute-start(bf16[1,3,441]{2,1,0:T(4,128)(2,1)S(1)} %collective-permute-done.12), channel_id=1, source_target_pairs={{0,16},{16,32},{32,48},{48,64},{64,80},{80,96},{96,112},{112,128},... | collective-permute-start | bytes 7946 | tf_op jit(solution)/shard_map/ppermute | solution.py:159
  100.6 6.9 %collective-permute-start.14 = (bf16[1,3,441]{2,1,0:T(4,128)(2,1)S(1)}, bf16[1,3,441]{2,1,0:T(4,128)(2,1)S(1)}, u32[]{:S(2)}, u32[]{:S(2)}) collective-permute-start(bf16[1,3,441]{2,1,0:T(4,128)(2,1)S(1)} %collective-permute-done.13), channel_id=1, source_target_pairs={{0,16},{16,32},{32,48},{48,64},{64,80},{80,96},{96,112},{112,128},... | collective-permute-start | bytes 7946 | tf_op jit(solution)/shard_map/ppermute | solution.py:159
  107.5 6.9 %collective-permute-start.15 = (bf16[1,3,441]{2,1,0:T(4,128)(2,1)S(1)}, bf16[1,3,441]{2,1,0:T(4,128)(2,1)S(1)}, u32[]{:S(2)}, u32[]{:S(2)}) collective-permute-start(bf16[1,3,441]{2,1,0:T(4,128)(2,1)S(1)} %collective-permute-done.14), channel_id=1, source_target_pairs={{0,16},{16,32},{32,48},{48,64},{64,80},{80,96},{96,112},{112,128},... | collective-permute-start | bytes 7946 | tf_op jit(solution)/shard_map/ppermute | solution.py:159
  114.5 7.0 %collective-permute-start.16 = (bf16[1,3,441]{2,1,0:T(4,128)(2,1)S(1)}, bf16[1,3,441]{2,1,0:T(4,128)(2,1)S(1)}, u32[]{:S(2)}, u32[]{:S(2)}) collective-permute-start(bf16[1,3,441]{2,1,0:T(4,128)(2,1)S(1)} %collective-permute-done.15), channel_id=1, source_target_pairs={{0,16},{16,32},{32,48},{48,64},{64,80},{80,96},{96,112},{112,128},... | collective-permute-start | bytes 7946 | tf_op jit(solution)/shard_map/ppermute | solution.py:159
  121.5 6.9 %collective-permute-start.17 = (bf16[1,3,441]{2,1,0:T(4,128)(2,1)S(1)}, bf16[1,3,441]{2,1,0:T(4,128)(2,1)S(1)}, u32[]{:S(2)}, u32[]{:S(2)}) collective-permute-start(bf16[1,3,441]{2,1,0:T(4,128)(2,1)S(1)} %collective-permute-done.16), channel_id=1, source_target_pairs={{0,16},{16,32},{32,48},{48,64},{64,80},{80,96},{96,112},{112,128},... | collective-permute-start | bytes 7946 | tf_op jit(solution)/shard_map/ppermute | solution.py:159
  128.4 6.9 %collective-permute-start.18 = (bf16[1,3,441]{2,1,0:T(4,128)(2,1)S(1)}, bf16[1,3,441]{2,1,0:T(4,128)(2,1)S(1)}, u32[]{:S(2)}, u32[]{:S(2)}) collective-permute-start(bf16[1,3,441]{2,1,0:T(4,128)(2,1)S(1)} %collective-permute-done.17), channel_id=1, source_target_pairs={{0,16},{16,32},{32,48},{48,64},{64,80},{80,96},{96,112},{112,128},... | collective-permute-start | bytes 7946 | tf_op jit(solution)/shard_map/ppermute | solution.py:159
  135.3 13.0 %collective-permute-start.19 = (bf16[1,3,441]{2,1,0:T(4,128)(2,1)S(1)}, bf16[1,3,441]{2,1,0:T(4,128)(2,1)S(1)}, u32[]{:S(2)}, u32[]{:S(2)}) collective-permute-start(bf16[1,3,441]{2,1,0:T(4,128)(2,1)S(1)} %collective-permute-done.18), channel_id=1, source_target_pairs={{0,16},{16,32},{32,48},{48,64},{64,80},{80,96},{96,112},{112,128},... | collective-permute-start | bytes 7946 | tf_op jit(solution)/shard_map/ppermute | solution.py:159
  156.9 33.1 %collective-permute-start.22 = (bf16[1,3,441]{2,1,0:T(4,128)(2,1)}, bf16[1,3,441]{2,1,0:T(4,128)(2,1)}, u32[]{:S(2)}, u32[]{:S(2)}) collective-permute-start(bf16[1,3,441]{2,1,0:T(4,128)(2,1)} %collective-permute-done.21), channel_id=1, source_target_pairs={{0,16},{16,32},{32,48},{48,64},{64,80},{80,96},{96,112},{112,128},... | collective-permute-start | bytes 7946 | tf_op jit(solution)/shard_map/ppermute | solution.py:159
  190.0 7.8 %collective-permute-start.23 = (bf16[1,3,441]{2,1,0:T(4,128)(2,1)}, bf16[1,3,441]{2,1,0:T(4,128)(2,1)}, u32[]{:S(2)}, u32[]{:S(2)}) collective-permute-start(bf16[1,3,441]{2,1,0:T(4,128)(2,1)} %collective-permute-done.22), channel_id=1, source_target_pairs={{0,16},{16,32},{32,48},{48,64},{64,80},{80,96},{96,112},{112,128},... | collective-permute-start | bytes 7946 | tf_op jit(solution)/shard_map/ppermute | solution.py:159
  320.0 7.7 %collective-permute-start.31 = (bf16[3,441]{1,0:T(4,128)(2,1)S(1)}, bf16[3,441]{1,0:T(4,128)(2,1)S(1)}, u32[]{:S(2)}, u32[]{:S(2)}) collective-permute-start(bf16[3,441]{1,0:T(4,128)(2,1)S(1)} %fusion.249), channel_id=1, source_target_pairs={{0,8},{8,0},{1,9},{9,1},{2,10},{10,2},{3,11},{11,3},{4,12},{12,4},... | collective-permute-start | bytes 7946 | tf_op jit(solution)/shard_map/ppermute | solution.py:37
  336.3 6.9 %collective-permute-start.34 = (bf16[1,3,441]{2,1,0:T(4,128)(2,1)S(1)}, bf16[1,3,441]{2,1,0:T(4,128)(2,1)S(1)}, u32[]{:S(2)}, u32[]{:S(2)}) collective-permute-start(bf16[1,3,441]{2,1,0:T(4,128)(2,1)S(1)} %collective-permute-done.33), channel_id=1, source_target_pairs={{0,16},{16,32},{32,48},{48,64},{64,80},{80,96},{96,112},{112,128},... | collective-permute-start | bytes 7946 | tf_op jit(solution)/shard_map/ppermute | solution.py:159
  343.2 6.9 %collective-permute-start.35 = (bf16[1,3,441]{2,1,0:T(4,128)(2,1)S(1)}, bf16[1,3,441]{2,1,0:T(4,128)(2,1)S(1)}, u32[]{:S(2)}, u32[]{:S(2)}) collective-permute-start(bf16[1,3,441]{2,1,0:T(4,128)(2,1)S(1)} %collective-permute-done.34), channel_id=1, source_target_pairs={{0,16},{16,32},{32,48},{48,64},{64,80},{80,96},{96,112},{112,128},... | collective-permute-start | bytes 7946 | tf_op jit(solution)/shard_map/ppermute | solution.py:159
  350.1 6.9 %collective-permute-start.36 = (bf16[1,3,441]{2,1,0:T(4,128)(2,1)S(1)}, bf16[1,3,441]{2,1,0:T(4,128)(2,1)S(1)}, u32[]{:S(2)}, u32[]{:S(2)}) collective-permute-start(bf16[1,3,441]{2,1,0:T(4,128)(2,1)S(1)} %collective-permute-done.35), channel_id=1, source_target_pairs={{0,16},{16,32},{32,48},{48,64},{64,80},{80,96},{96,112},{112,128},... | collective-permute-start | bytes 7946 | tf_op jit(solution)/shard_map/ppermute | solution.py:159
  357.1 6.9 %collective-permute-start.37 = (bf16[1,3,441]{2,1,0:T(4,128)(2,1)S(1)}, bf16[1,3,441]{2,1,0:T(4,128)(2,1)S(1)}, u32[]{:S(2)}, u32[]{:S(2)}) collective-permute-start(bf16[1,3,441]{2,1,0:T(4,128)(2,1)S(1)} %collective-permute-done.36), channel_id=1, source_target_pairs={{0,16},{16,32},{32,48},{48,64},{64,80},{80,96},{96,112},{112,128},... | collective-permute-start | bytes 7946 | tf_op jit(solution)/shard_map/ppermute | solution.py:159
  364.0 6.9 %collective-permute-start.38 = (bf16[1,3,441]{2,1,0:T(4,128)(2,1)S(1)}, bf16[1,3,441]{2,1,0:T(4,128)(2,1)S(1)}, u32[]{:S(2)}, u32[]{:S(2)}) collective-permute-start(bf16[1,3,441]{2,1,0:T(4,128)(2,1)S(1)} %collective-permute-done.37), channel_id=1, source_target_pairs={{0,16},{16,32},{32,48},{48,64},{64,80},{80,96},{96,112},{112,128},... | collective-permute-start | bytes 7946 | tf_op jit(solution)/shard_map/ppermute | solution.py:159
  370.9 7.4 %collective-permute-start.39 = (bf16[1,3,441]{2,1,0:T(4,128)(2,1)S(1)}, bf16[1,3,441]{2,1,0:T(4,128)(2,1)S(1)}, u32[]{:S(2)}, u32[]{:S(2)}) collective-permute-start(bf16[1,3,441]{2,1,0:T(4,128)(2,1)S(1)} %collective-permute-done.38), channel_id=1, source_target_pairs={{0,16},{16,32},{32,48},{48,64},{64,80},{80,96},{96,112},{112,128},... | collective-permute-start | bytes 7946 | tf_op jit(solution)/shard_map/ppermute | solution.py:159
  378.3 12.4 %collective-permute-start.40 = (bf16[1,3,441]{2,1,0:T(4,128)(2,1)S(1)}, bf16[1,3,441]{2,1,0:T(4,128)(2,1)S(1)}, u32[]{:S(2)}, u32[]{:S(2)}) collective-permute-start(bf16[1,3,441]{2,1,0:T(4,128)(2,1)S(1)} %collective-permute-done.39), channel_id=1, source_target_pairs={{0,16},{16,32},{32,48},{48,64},{64,80},{80,96},{96,112},{112,128},... | collective-permute-start | bytes 7946 | tf_op jit(solution)/shard_map/ppermute | solution.py:159
  385.2 92.4 %collective-permute-start.27 = (bf16[6,1,64,128]{3,2,1,0:T(8,128)(2,1)}, bf16[6,1,64,128]{3,2,1,0:T(8,128)(2,1)}, u32[]{:S(2)}, u32[]{:S(2)}) collective-permute-start(bf16[6,1,64,128]{3,2,1,0:T(8,128)(2,1)} %pad_maximum_fusion.2), channel_id=1, source_target_pairs={{16,0},{32,16},{48,32},{64,48},{80,64},{96,80},{112,96},{128,112},... | collective-permute-start | bytes 294920 | tf_op jit(solution)/shard_map/ppermute | solution.py:25
  385.3 92.3 %collective-permute-start.26 = (bf16[6,1,64,128]{3,2,1,0:T(8,128)(2,1)}, bf16[6,1,64,128]{3,2,1,0:T(8,128)(2,1)}, u32[]{:S(2)}, u32[]{:S(2)}) collective-permute-start(bf16[6,1,64,128]{3,2,1,0:T(8,128)(2,1)} %pad_maximum_fusion.2), channel_id=1, source_target_pairs={{0,16},{16,32},{32,48},{48,64},{64,80},{80,96},{96,112},{112,128},... | collective-permute-start | bytes 294920 | tf_op jit(solution)/shard_map/ppermute | solution.py:24
  394.3 9.7 %collective-permute-start.42 = (bf16[1,3,441]{2,1,0:T(4,128)(2,1)S(1)}, bf16[1,3,441]{2,1,0:T(4,128)(2,1)S(1)}, u32[]{:S(2)}, u32[]{:S(2)}) collective-permute-start(bf16[1,3,441]{2,1,0:T(4,128)(2,1)S(1)} %collective-permute-done.41), channel_id=1, source_target_pairs={{0,16},{16,32},{32,48},{48,64},{64,80},{80,96},{96,112},{112,128},... | collective-permute-start | bytes 7946 | tf_op jit(solution)/shard_map/ppermute | solution.py:159
  399.6 13.3 %collective-permute-start.25 = (bf16[6,1,1,128]{3,2,1,0:T(2,128)(2,1)S(1)}, bf16[6,1,1,128]{3,2,1,0:T(2,128)(2,1)S(1)}, u32[]{:S(2)}, u32[]{:S(2)}) collective-permute-start(bf16[6,1,1,128]{3,2,1,0:T(2,128)(2,1)S(1)} %get-tuple-element.180), channel_id=1, source_target_pairs={{1,0},{2,1},{3,2},{4,3},{5,4},{6,5},{7,6},{8,7},{9,8},{10,9},{11,1... | collective-permute-start | bytes 4616 | tf_op jit(solution)/shard_map/ppermute | solution.py:25
  400.9 12.0 %collective-permute-start.24 = (bf16[6,1,1,128]{3,2,1,0:T(2,128)(2,1)S(1)}, bf16[6,1,1,128]{3,2,1,0:T(2,128)(2,1)S(1)}, u32[]{:S(2)}, u32[]{:S(2)}) collective-permute-start(bf16[6,1,1,128]{3,2,1,0:T(2,128)(2,1)S(1)} %get-tuple-element.179), channel_id=1, source_target_pairs={{0,1},{1,2},{2,3},{3,4},{4,5},{5,6},{6,7},{7,8},{8,9},{9,10},{10,1... | collective-permute-start | bytes 4616 | tf_op jit(solution)/shard_map/ppermute | solution.py:24
  404.0 6.4 %collective-permute-start.43 = (bf16[1,3,441]{2,1,0:T(4,128)(2,1)S(1)}, bf16[1,3,441]{2,1,0:T(4,128)(2,1)S(1)}, u32[]{:S(2)}, u32[]{:S(2)}) collective-permute-start(bf16[1,3,441]{2,1,0:T(4,128)(2,1)S(1)} %collective-permute-done.42), channel_id=1, source_target_pairs={{0,16},{16,32},{32,48},{48,64},{64,80},{80,96},{96,112},{112,128},... | collective-permute-start | bytes 7946 | tf_op jit(solution)/shard_map/ppermute | solution.py:159
  414.3 6.9 %collective-permute-start.45 = (bf16[1,3,441]{2,1,0:T(4,128)(2,1)S(1)}, bf16[1,3,441]{2,1,0:T(4,128)(2,1)S(1)}, u32[]{:S(2)}, u32[]{:S(2)}) collective-permute-start(bf16[1,3,441]{2,1,0:T(4,128)(2,1)S(1)} %collective-permute-done.44), channel_id=1, source_target_pairs={{0,16},{16,32},{32,48},{48,64},{64,80},{80,96},{96,112},{112,128},... | collective-permute-start | bytes 7946 | tf_op jit(solution)/shard_map/ppermute | solution.py:159
  421.2 31.2 %collective-permute-start.46 = (bf16[1,3,441]{2,1,0:T(4,128)(2,1)S(1)}, bf16[1,3,441]{2,1,0:T(4,128)(2,1)S(1)}, u32[]{:S(2)}, u32[]{:S(2)}) collective-permute-start(bf16[1,3,441]{2,1,0:T(4,128)(2,1)S(1)} %collective-permute-done.45), channel_id=1, source_target_pairs={{0,16},{16,32},{32,48},{48,64},{64,80},{80,96},{96,112},{112,128},... | collective-permute-start | bytes 7946 | tf_op jit(solution)/shard_map/ppermute | solution.py:159
  (89 other events, 1382.6 us)
